TPU v7x, 256 devices: a whole 4x4x8 slice. The times are simulated.
256 devices in a mesh: rows: 64 (over x, z, core), cols: 4 (over y).
Axes of the slice: x: 4, y: 4, z: 8, core: 2. Of those that a mesh axis runs over, the one named last changes fastest.
Arguments:
- kernel: float32 [16384, 16384], P('rows', 'cols'), may hold values from 0 to 2, as said below
- row_block: int32 [256], P('rows'), may hold values from 0 to 255, as said below
- panel_order: int32 [2], replicated, may hold values from 0 to 63, as said below
- samples: float32 [16384, 512], P('rows', 'cols'), may hold values from -6 to 6
Outputs:
- trailing: float32 [16384, 16384], P('rows', 'cols')
- factor: float32 [16384, 512], P('rows')
- solved: float32 [512, 512], P(None, 'cols')
- reduced_samples: float32 [16384, 512], P('rows', 'cols')
Inputs may be any that keep to these rules, and one draw needn't show every extreme that they name: `row_block`: the stored row blocks of rows index i (stored blocks i * 4 to (i + 1) * 4 - 1) hold the global row blocks i + t * 64, t = 0 .. 3, each once, in some order. `panel_order`: the entries are distinct, and one of them is 63. `kernel`: in global row order the matrix is symmetric and positive definite, its smallest eigenvalue 0.25 or more.
All inputs are finite; a program needn't handle non-finite values.
Results may differ from a plain program's by a relative error of at most 0.0003.
Values sent between devices are 32-bit elements; how exact they have to be, the bound alone decides.
No kernel may reach another device: no remote copies, remote signals or barrier semaphores. Data moves between devices by JAX's collectives and lax.ppermute only.
A program may use at most 128 MiB of HBM per device.

v0:
```python
import jax
import jax.numpy as jnp
from jax import lax
from jax.sharding import PartitionSpec as P

PW = 256
PANELS = 2
EXACT = lax.Precision.HIGHEST


def broadcast(block, axis, owner):
    block = jnp.where(lax.axis_index(axis) == owner, block, jnp.zeros_like(block))
    return lax.psum(block, axis)


def times_transposed(left_side, right_side):
    return lax.dot_general(
        left_side,
        right_side,
        (((1,), (1,)), ((), ())),
        precision=EXACT,
        preferred_element_type=jnp.float32,
    )


def matmul_plain(left_side, right_side):
    return jnp.dot(left_side, right_side, precision=EXACT, preferred_element_type=jnp.float32)


def stored_order(array, restore, blocks_here):
    width_here = array.shape[1]
    return jnp.take(array.reshape(blocks_here, -1, width_here), restore, axis=0).reshape(
        array.shape
    )


def on_device(kernel, row_block, panel_order, samples):
    rows_count = lax.axis_size("rows")
    cols_count = lax.axis_size("cols")
    cols_place = lax.axis_index("cols")
    blocks_here = row_block.shape[0]
    local_rows, local_cols = kernel.shape
    block_rows = local_rows // blocks_here
    per_panel = PW // block_rows
    share = blocks_here // cols_count
    right_cols = samples.shape[1]
    ranking = jnp.argsort(row_block)
    restore = jnp.argsort(ranking)
    sorted_blocks = jnp.take(row_block, ranking)
    trailing_work = jnp.take(
        kernel.reshape(blocks_here, block_rows, local_cols), ranking, axis=0
    ).reshape(local_rows, local_cols)
    right_side = jnp.take(
        samples.reshape(blocks_here, block_rows, right_cols), ranking, axis=0
    ).reshape(local_rows, right_cols)
    identity = jnp.eye(PW, dtype=jnp.float32)
    factors = []
    solutions = []
    for panel_step in range(PANELS):
        panel_start = panel_order[panel_step] * PW
        column_owner = panel_start // local_cols
        offset = panel_start - column_owner * local_cols
        own_columns = lax.dynamic_slice_in_dim(trailing_work, offset, PW, 1)
        columns = broadcast(own_columns, "cols", column_owner)
        first_block = panel_order[panel_step] * per_panel
        wanted = first_block + jnp.arange(per_panel, dtype=jnp.int32)
        chooser = (wanted[:, None] == sorted_blocks[None, :]).astype(jnp.float32)
        diag_part = jnp.einsum(
            "ot,trp->orp", chooser, columns.reshape(blocks_here, block_rows, PW), precision=EXACT
        ).reshape(PW, PW)
        right_part = jnp.einsum(
            "ot,trp->orp",
            chooser,
            right_side.reshape(blocks_here, block_rows, right_cols),
            precision=EXACT,
        ).reshape(PW, right_cols)
        diagonal, panel_right = lax.psum((diag_part, right_part), "rows")
        lower_factor = jnp.linalg.cholesky(diagonal)
        inverse = jax.scipy.linalg.solve_triangular(lower_factor, identity, lower=True)
        factor_own = times_transposed(columns, inverse)
        solved_now = matmul_plain(inverse, panel_right)
        right_side = right_side - matmul_plain(factor_own, solved_now)
        my_piece = lax.dynamic_slice_in_dim(
            factor_own, cols_place * share * block_rows, share * block_rows, 0
        )
        spread = times_transposed(factor_own, lax.all_gather(my_piece, "rows", axis=0, tiled=True))
        update = (
            spread.reshape(local_rows, rows_count, share, block_rows)
            .transpose(0, 2, 1, 3)
            .reshape(local_rows, local_cols)
        )
        trailing_work = trailing_work - update
        factors.append(factor_own)
        solutions.append(solved_now)
    factor_all = jnp.concatenate(factors, 1)
    return (
        stored_order(trailing_work, restore, blocks_here),
        stored_order(factor_all, restore, blocks_here),
        jnp.concatenate(solutions, 0),
        stored_order(right_side, restore, blocks_here),
    )


def solution(mesh):
    in_specs = (P("rows", "cols"), P("rows"), P(), P("rows", "cols"))
    out_specs = (P("rows", "cols"), P("rows", None), P(None, "cols"), P("rows", "cols"))
    return jax.shard_map(
        on_device, mesh=mesh, in_specs=in_specs, out_specs=out_specs, check_vma=False
    )
```

profile of v0, /device:TPU:1, one launch (start us, length us, event | category | flops | bytes accessed | tf_op | source)
XLA Modules:
  0.0 816.9 jit_solution(4630192233342211881)
XLA Ops:
  7.2 1.3 fusion.51
  9.2 1.4 sort.31
  10.6 1.3 gather_fusion
  11.9 5.0 gather_fusion.2
  16.9 2.7 broadcast_select_fusion.1
  19.6 2.0 copy-done.2
  21.6 0.7 dynamic-slice_select_fusion.1
  24.0 0.7 copy.24
  24.7 46.3 %all-reduce.8.cloned.1.call-done = f32[256,256]{1,0:T(8,128)} async-done(((f32[256,256]{1,0:T(8,128)}), f32[256,256]{1,0:T(8,128)}) %all-reduce.8.cloned.1.call-update) | async-done | bytes 262160 | tf_op jit(solution)/shard_map/psum | solution.py:13
  71.0 1.5 fusion.4
  72.6 0.8 copy.17
  73.6 183.5 %all-reduce.14.cloned.1.call-done = (f32[256,256]{0,1:T(8,128)}, f32[256,128]{1,0:T(8,128)}) async-done(((f32[256,256]{0,1:T(8,128)}, f32[256,128]{1,0:T(8,128)}), (f32[256,256]{0,1:T(8,128)}, f32[256,128]{1,0:T(8,128)})) %all-reduce.14.cloned.1.call-update) | async-done | bytes 393232 | tf_op jit(solution)/shard_map/psum | solution.py:77
  257.1 1.1 copy.18
  258.2 1.0 fusion.1
  259.2 11.7 %cholesky.130 = f32[128,128]{1,0:T(8,128)S(1)} custom-call(f32[128,128]{1,0:T(8,128)S(1)} %cholesky.194), custom_call_target="Cholesky" | custom-call | tf_op jit(solution)/shard_map/jit(cholesky)/cholesky | solution.py:78
  271.0 9.8 %custom-call.13 = f32[1,128,128]{1,2,0:T(8,128)S(1)} custom-call(f32[1,128,128]{2,1,0:T(8,128)S(1)} %get-tuple-element.61), custom_call_target="InvertDiagBlocksLowerTriangular" | custom-call | tf_op jit(solution)/shard_map/jit(cholesky)/cholesky | solution.py:78
  281.3 11.7 %cholesky.147 = f32[128,128]{1,0:T(8,128)S(1)} custom-call(f32[128,128]{1,0:T(8,128)S(1)} %convolution_subtract_fusion.7), custom_call_target="Cholesky" | custom-call | tf_op jit(solution)/shard_map/jit(cholesky)/cholesky | solution.py:78
  293.1 0.6 compare_reduce_fusion.2
  295.1 4.5 while.4
  296.2 1.4 bitcast_dynamic-update-slice_fusion.4
  298.2 1.4 bitcast_dynamic-update-slice_fusion.4
  299.6 19.7 %custom-call.14 = f32[2,128,128]{1,2,0:T(8,128)S(1)} custom-call(f32[2,128,128]{2,1,0:T(8,128)S(1)} %get-tuple-element.26), custom_call_target="InvertDiagBlocksLowerTriangular" | custom-call | tf_op jit(solution)/shard_map/jit(_solve_triangular)/triangular_solve | solution.py:79
  323.1 78.1 %all-gather.3.cloned.1.call-done = f32[4096,256]{1,0:T(8,128)} async-done(((f32[64,256]{1,0:T(8,128)}), f32[4096,256]{1,0:T(8,128)}) %all-gather.3.cloned.1.call-update) | async-done | bytes 4194320 | tf_op jit(solution)/shard_map/all_gather | solution.py:86
  401.1 11.4 %convolution_subtract_fusion.1 = f32[256,4096]{1,0:T(8,128)S(1)} fusion(f32[256,4096]{1,0:T(8,128)} %bitcast.108, f32[256,256]{1,0:T(8,128)S(1)} %fusion.10, f32[4096,256]{1,0:T(8,128)} %all-gather.3.cloned.1.call-done), kind=kOutput, calls=%fused_computation.11 | convolution fusion | flops 3222274048 | bytes 12845056 | tf_op jit(solution)/shard_map/dot_general | solution.py:17
  412.6 2.0 copy-done.1
  414.6 0.7 dynamic-slice_select_fusion
  416.1 0.7 copy.26
  416.8 40.3 %all-reduce.10.cloned.1.call-done = f32[256,256]{1,0:T(8,128)} async-done(((f32[256,256]{1,0:T(8,128)}), f32[256,256]{1,0:T(8,128)}) %all-reduce.10.cloned.1.call-update) | async-done | bytes 262160 | tf_op jit(solution)/shard_map/psum | solution.py:13
  457.1 1.5 fusion.2
  458.7 0.8 copy.21
  459.8 183.3 %all-reduce.12.cloned.1.call-done = (f32[256,256]{0,1:T(8,128)}, f32[256,128]{1,0:T(8,128)}) async-done(((f32[256,256]{0,1:T(8,128)}, f32[256,128]{1,0:T(8,128)}), (f32[256,256]{0,1:T(8,128)}, f32[256,128]{1,0:T(8,128)})) %all-reduce.12.cloned.1.call-update) | async-done | bytes 393232 | tf_op jit(solution)/shard_map/psum | solution.py:77
  643.0 1.1 copy.22
  644.2 1.0 fusion
  645.2 11.7 %cholesky.164 = f32[128,128]{1,0:T(8,128)S(1)} custom-call(f32[128,128]{1,0:T(8,128)S(1)} %cholesky.197), custom_call_target="Cholesky" | custom-call | tf_op jit(solution)/shard_map/jit(cholesky)/cholesky | solution.py:78
  656.9 9.8 %custom-call.15 = f32[1,128,128]{1,2,0:T(8,128)S(1)} custom-call(f32[1,128,128]{2,1,0:T(8,128)S(1)} %get-tuple-element.57), custom_call_target="InvertDiagBlocksLowerTriangular" | custom-call | tf_op jit(solution)/shard_map/jit(cholesky)/cholesky | solution.py:78
  667.2 11.7 %cholesky.181 = f32[128,128]{1,0:T(8,128)S(1)} custom-call(f32[128,128]{1,0:T(8,128)S(1)} %convolution_subtract_fusion.6), custom_call_target="Cholesky" | custom-call | tf_op jit(solution)/shard_map/jit(cholesky)/cholesky | solution.py:78
  681.6 4.2 while.5
  682.4 1.4 bitcast_dynamic-update-slice_fusion.5
  684.4 1.4 bitcast_dynamic-update-slice_fusion.5
  685.8 19.7 %custom-call.16 = f32[2,128,128]{1,2,0:T(8,128)S(1)} custom-call(f32[2,128,128]{2,1,0:T(8,128)S(1)} %get-tuple-element.27), custom_call_target="InvertDiagBlocksLowerTriangular" | custom-call | tf_op jit(solution)/shard_map/jit(_solve_triangular)/triangular_solve | solution.py:79
  707.5 0.7 sort.32
  710.4 0.7 pad_maximum_fusion.3
  711.2 0.7 broadcast_select_fusion.2
  711.9 0.9 bitcast_select_fusion
  712.8 74.6 %all-gather.5.cloned.1.call-done = f32[4096,256]{1,0:T(8,128)} async-done(((f32[64,256]{1,0:T(8,128)}), f32[4096,256]{1,0:T(8,128)}) %all-gather.5.cloned.1.call-update) | async-done | bytes 4194320 | tf_op jit(solution)/shard_map/all_gather | solution.py:86
  787.4 12.7 %convolution_subtract_fusion = f32[256,4096]{1,0:T(8,128)} fusion(f32[256,4096]{1,0:T(8,128)} %copy-done.1, f32[256,256]{1,0:T(8,128)S(1)} %fusion.8, f32[4096,256]{1,0:T(8,128)} %all-gather.5.cloned.1.call-done), kind=kOutput, calls=%fused_computation.10 | convolution fusion | flops 3222274048 | bytes 12845056 | tf_op jit(solution)/shard_map/dot_general | solution.py:17
  800.1 4.9 gather_fusion.3
  805.0 4.8 broadcast_select_fusion
  (88 shorter events, 13.7 us)
Async XLA Ops:
  7.2 15.9 %copy-start = (f32[256,128]{1,0:T(8,128)S(1)}, f32[256,128]{1,0:T(8,128)}, u32[]{:S(2)}) copy-start(f32[256,128]{1,0:T(8,128)} %param.14) | copy-start | bytes 393220
  7.2 63.8 %all-reduce.8.cloned.1.call-start = ((), (), s32[]{:S(2)}) async-start(), calls=%async_computation | async-start | bytes 524288 | tf_op jit(solution)/shard_map/psum | solution.py:13
  19.6 2.0 copy-start.2
  22.4 234.8 %all-reduce.14.cloned.1.call-start = ((), (), s32[]{:S(2)}) async-start(), calls=%async_computation.5 | async-start | bytes 786432 | tf_op jit(solution)/shard_map/psum | solution.py:77
  71.0 249.2 %copy-start.3 = (f32[256,256]{1,0:T(8,128)S(1)}, f32[256,256]{1,0:T(8,128)}, u32[]{:S(2)}) copy-start(f32[256,256]{1,0:T(8,128)} %all-reduce.8.cloned.1.call-done) | copy-start | bytes 786436
  73.5 327.7 %all-gather.3.cloned.1.call-start = ((), (), s32[]{:S(2)}) async-start(), calls=%async_computation.1 | async-start | bytes 4259840 | tf_op jit(solution)/shard_map/all_gather | solution.py:86
  257.1 65.6 %copy-start.5 = (f32[256,128]{1,0:T(8,128)S(1)}, f32[256,128]{1,0:T(8,128)}, u32[]{:S(2)}) copy-start(f32[256,128]{1,0:T(8,128)} %get-tuple-element.47) | copy-start | bytes 393220
  321.3 135.8 %all-reduce.10.cloned.1.call-start = ((), (), s32[]{:S(2)}) async-start(), calls=%async_computation.2 | async-start | bytes 524288 | tf_op jit(solution)/shard_map/psum | solution.py:13
  412.6 2.0 copy-start.1
  415.3 227.7 %all-reduce.12.cloned.1.call-start = ((), (), s32[]{:S(2)}) async-start(), calls=%async_computation.4 | async-start | bytes 786432 | tf_op jit(solution)/shard_map/psum | solution.py:77
  457.1 249.3 %copy-start.4 = (f32[256,256]{1,0:T(8,128)S(1)}, f32[256,256]{1,0:T(8,128)}, u32[]{:S(2)}) copy-start(f32[256,256]{1,0:T(8,128)} %all-reduce.10.cloned.1.call-done) | copy-start | bytes 786436
  459.5 327.8 %all-gather.5.cloned.1.call-start = ((), (), s32[]{:S(2)}) async-start(), calls=%async_computation.3 | async-start | bytes 4259840 | tf_op jit(solution)/shard_map/all_gather | solution.py:86
  643.0 65.4 %copy-start.6 = (f32[256,128]{1,0:T(8,128)S(1)}, f32[256,128]{1,0:T(8,128)}, u32[]{:S(2)}) copy-start(f32[256,128]{1,0:T(8,128)} %get-tuple-element.45) | copy-start | bytes 393220
Sparse Core Ops, SparseCore 0:
  22.5 48.4 all-reduce.7
  75.5 181.5 all-reduce.13
  321.4 79.7 all-gather.2
  415.5 41.5 all-reduce.9
  461.4 181.5 all-reduce.11
  707.6 79.7 all-gather.4
where the time goes:
time: 826 us; the launch traced here: 817 us
  waiting for transfers between devices  606 us (73%)
  other arithmetic  124 us (15%)
  local copies, waits for them, and re-layouts  33.1 us (4%)
  matrix products  32.9 us (4%)
  between operations  20 us (2%)
    psum x2, waiting for transfers between devices, on_device(): diagonal, panel_right = lax.psum((diag_part, right_part), 'rows')  367 us
    all_gather x2, waiting for transfers between devices, on_device(): lax.all_gather(my_piece, 'rows', axis=0, tiled=True)  153 us
    psum x2, waiting for transfers between devices, broadcast(): return lax.psum(block, axis)  86.6 us
    another operation x13, other arithmetic, on_device(): lower_factor = jnp.linalg.cholesky(diagonal)  68.5 us
    another operation x5, other arithmetic, on_device(): jax.scipy.linalg.solve_triangular(lower_factor, identity, lower=True)  39.4 us
    dot_general x4, matrix products, times_transposed(): lax.dot_general(left_side, right_side, (((1,), (1,)), ((), ())), precisio...  25 us
  transfers between devices with their start and end apart: 6, of which 6 were waited for; matrix products, arithmetic and copies ran while one was open for 1% of the time, Pallas kernels for 0%

commit v1 on v0

--- a/solution.py
+++ b/solution.py
@@ -6,6 +6,12 @@
 PW = 256
 PANELS = 2
 EXACT = lax.Precision.HIGHEST
+
+
+def tiled_gather(x, axis, dim):
+    size = lax.axis_size(axis)
+    repeats = [size if d == dim else 1 for d in range(x.ndim)]
+    return lax.all_to_all(jnp.tile(x, repeats), axis, split_axis=dim, concat_axis=dim, tiled=True)
 
 
 def broadcast(block, axis, owner):
@@ -83,7 +89,7 @@
         my_piece = lax.dynamic_slice_in_dim(
             factor_own, cols_place * share * block_rows, share * block_rows, 0
         )
-        spread = times_transposed(factor_own, lax.all_gather(my_piece, "rows", axis=0, tiled=True))
+        spread = times_transposed(factor_own, tiled_gather(my_piece, "rows", 0))
         update = (
             spread.reshape(local_rows, rows_count, share, block_rows)
             .transpose(0, 2, 1, 3)

time: 826 us -> 881 us (1.067)
  waiting for transfers between devices: 606 us -> 638 us
  starting transfers between devices: 0.42 us -> 20.3 us
    all_to_all x0 -> x2, waiting for transfers between devices: none -> 185 us  [tiled_gather(): lax.all_to_all(jnp.tile(x, repeats), axis, split_axis=dim, concat_axis=di...]
    all_gather x2 -> x0, waiting for transfers between devices: 153 us -> none  [on_device(): lax.all_gather(my_piece, 'rows', axis=0, tiled=True)]
    all_to_all x0 -> x2, starting transfers between devices: none -> 19.9 us  [tiled_gather(): lax.all_to_all(jnp.tile(x, repeats), axis, split_axis=dim, concat_axis=di...]
where the time goes in v1:
time: 881 us; the launch traced here: 872 us
  waiting for transfers between devices  638 us (72%)
  other arithmetic  124 us (14%)
  local copies, waits for them, and re-layouts  36.7 us (4%)
  matrix products  32.9 us (4%)
  starting transfers between devices  20.3 us (2%)
  between operations  19.7 us (2%)
    psum x2, waiting for transfers between devices, on_device(): diagonal, panel_right = lax.psum((diag_part, right_part), 'rows')  367 us
    all_to_all x2, waiting for transfers between devices, tiled_gather(): lax.all_to_all(jnp.tile(x, repeats), axis, split_axis=dim, concat_axis=di...  185 us
    psum x2, waiting for transfers between devices, broadcast(): return lax.psum(block, axis)  85.9 us
    another operation x13, other arithmetic, on_device(): lower_factor = jnp.linalg.cholesky(diagonal)  68.5 us
    another operation x5, other arithmetic, on_device(): jax.scipy.linalg.solve_triangular(lower_factor, identity, lower=True)  39.4 us
    dot_general x4, matrix products, times_transposed(): lax.dot_general(left_side, right_side, (((1,), (1,)), ((), ())), precisio...  25 us
    all_to_all x2, starting transfers between devices, tiled_gather(): lax.all_to_all(jnp.tile(x, repeats), axis, split_axis=dim, concat_axis=di...  19.9 us
  transfers between devices with their start and end apart: 6, of which 6 were waited for; matrix products, arithmetic and copies ran while one was open for 1% of the time, Pallas kernels for 0%

profile of v1, /device:TPU:1, one launch (start us, length us, event | category | flops | bytes accessed | tf_op | source)
XLA Modules:
  0.0 871.7 jit_solution(16290925665993457061)
XLA Ops:
  7.2 1.3 fusion.51
  9.2 1.4 sort.31
  10.6 1.3 gather_fusion
  11.9 5.0 gather_fusion.2
  16.9 2.7 broadcast_select_fusion.1
  19.6 2.0 copy-done.2
  21.6 0.7 dynamic-slice_select_fusion.1
  24.7 46.3 %all-reduce.8.cloned.1.call-done = f32[256,256]{1,0:T(8,128)} async-done(((f32[256,256]{1,0:T(8,128)}), f32[256,256]{1,0:T(8,128)}) %all-reduce.8.cloned.1.call-update) | async-done | bytes 262160 | tf_op jit(solution)/shard_map/psum | solution.py:19
  71.0 1.5 fusion.4
  72.6 0.8 copy.17
  73.5 183.6 %all-reduce.14.cloned.1.call-done = (f32[256,256]{0,1:T(8,128)}, f32[256,128]{1,0:T(8,128)}) async-done(((f32[256,256]{0,1:T(8,128)}, f32[256,128]{1,0:T(8,128)}), (f32[256,256]{0,1:T(8,128)}, f32[256,128]{1,0:T(8,128)})) %all-reduce.14.cloned.1.call-update) | async-done | bytes 393232 | tf_op jit(solution)/shard_map/psum | solution.py:83
  257.1 1.1 copy.18
  258.2 1.0 fusion.1
  259.2 11.7 %cholesky.130 = f32[128,128]{1,0:T(8,128)S(1)} custom-call(f32[128,128]{1,0:T(8,128)S(1)} %cholesky.194), custom_call_target="Cholesky" | custom-call | tf_op jit(solution)/shard_map/jit(cholesky)/cholesky | solution.py:84
  271.0 9.8 %custom-call.13 = f32[1,128,128]{1,2,0:T(8,128)S(1)} custom-call(f32[1,128,128]{2,1,0:T(8,128)S(1)} %get-tuple-element.61), custom_call_target="InvertDiagBlocksLowerTriangular" | custom-call | tf_op jit(solution)/shard_map/jit(cholesky)/cholesky | solution.py:84
  281.3 11.7 %cholesky.147 = f32[128,128]{1,0:T(8,128)S(1)} custom-call(f32[128,128]{1,0:T(8,128)S(1)} %convolution_subtract_fusion.7), custom_call_target="Cholesky" | custom-call | tf_op jit(solution)/shard_map/jit(cholesky)/cholesky | solution.py:84
  295.1 4.5 while.4
  296.2 1.4 bitcast_dynamic-update-slice_fusion.4
  298.2 1.4 bitcast_dynamic-update-slice_fusion.4
  299.6 19.7 %custom-call.14 = f32[2,128,128]{1,2,0:T(8,128)S(1)} custom-call(f32[2,128,128]{2,1,0:T(8,128)S(1)} %get-tuple-element.26), custom_call_target="InvertDiagBlocksLowerTriangular" | custom-call | tf_op jit(solution)/shard_map/jit(_solve_triangular)/triangular_solve | solution.py:85
  320.6 2.5 tile.4
  323.1 10.0 %all-to-all-start = ((f32[64,64,256]{2,1,0:T(8,128)}), f32[64,64,256]{2,1,0:T(8,128)}, u32[]{:S(2)}, u32[]{:S(2)}) async-start(f32[64,64,256]{2,1,0:T(8,128)} %tile.4), calls=%async_computation | async-start | bytes 8388608 | tf_op jit(solution)/shard_map/all_to_all | solution.py:14
  334.8 94.1 %all-to-all-done = f32[64,64,256]{2,1,0:T(8,128)} async-done(((f32[64,64,256]{2,1,0:T(8,128)}), f32[64,64,256]{2,1,0:T(8,128)}, u32[]{:S(2)}, u32[]{:S(2)}) %all-to-all-start) | async-done | bytes 4194336 | tf_op jit(solution)/shard_map/all_to_all | solution.py:14
  428.9 11.4 %convolution_subtract_fusion.1 = f32[256,4096]{1,0:T(8,128)S(1)} fusion(f32[256,4096]{1,0:T(8,128)} %bitcast.110, f32[256,256]{1,0:T(8,128)S(1)} %fusion.10, f32[4096,256]{1,0:T(8,128)} %bitcast.12), kind=kOutput, calls=%fused_computation.11 | convolution fusion | flops 3222274048 | bytes 12845056 | tf_op jit(solution)/shard_map/dot_general | solution.py:23
  440.4 2.0 copy-done.1
  442.4 0.7 dynamic-slice_select_fusion
  444.7 39.6 %all-reduce.10.cloned.1.call-done = f32[256,256]{1,0:T(8,128)} async-done(((f32[256,256]{1,0:T(8,128)}), f32[256,256]{1,0:T(8,128)}) %all-reduce.10.cloned.1.call-update) | async-done | bytes 262160 | tf_op jit(solution)/shard_map/psum | solution.py:19
  484.4 1.5 fusion.2
  486.0 0.8 copy.21
  486.9 183.5 %all-reduce.12.cloned.1.call-done = (f32[256,256]{0,1:T(8,128)}, f32[256,128]{1,0:T(8,128)}) async-done(((f32[256,256]{0,1:T(8,128)}, f32[256,128]{1,0:T(8,128)}), (f32[256,256]{0,1:T(8,128)}, f32[256,128]{1,0:T(8,128)})) %all-reduce.12.cloned.1.call-update) | async-done | bytes 393232 | tf_op jit(solution)/shard_map/psum | solution.py:83
  670.3 1.1 copy.22
  671.4 1.0 fusion
  672.4 11.7 %cholesky.164 = f32[128,128]{1,0:T(8,128)S(1)} custom-call(f32[128,128]{1,0:T(8,128)S(1)} %cholesky.197), custom_call_target="Cholesky" | custom-call | tf_op jit(solution)/shard_map/jit(cholesky)/cholesky | solution.py:84
  684.2 9.8 %custom-call.15 = f32[1,128,128]{1,2,0:T(8,128)S(1)} custom-call(f32[1,128,128]{2,1,0:T(8,128)S(1)} %get-tuple-element.57), custom_call_target="InvertDiagBlocksLowerTriangular" | custom-call | tf_op jit(solution)/shard_map/jit(cholesky)/cholesky | solution.py:84
  694.5 11.7 %cholesky.181 = f32[128,128]{1,0:T(8,128)S(1)} custom-call(f32[128,128]{1,0:T(8,128)S(1)} %convolution_subtract_fusion.6), custom_call_target="Cholesky" | custom-call | tf_op jit(solution)/shard_map/jit(cholesky)/cholesky | solution.py:84
  708.9 4.2 while.5
  709.7 1.4 bitcast_dynamic-update-slice_fusion.5
  711.7 1.4 bitcast_dynamic-update-slice_fusion.5
  713.1 19.7 %custom-call.16 = f32[2,128,128]{1,2,0:T(8,128)S(1)} custom-call(f32[2,128,128]{2,1,0:T(8,128)S(1)} %get-tuple-element.27), custom_call_target="InvertDiagBlocksLowerTriangular" | custom-call | tf_op jit(solution)/shard_map/jit(_solve_triangular)/triangular_solve | solution.py:85
  734.1 2.5 tile.5
  736.6 10.0 %all-to-all-start.1 = ((f32[64,64,256]{2,1,0:T(8,128)}), f32[64,64,256]{2,1,0:T(8,128)}, u32[]{:S(2)}, u32[]{:S(2)}) async-start(f32[64,64,256]{2,1,0:T(8,128)} %tile.5), calls=%async_computation.1 | async-start | bytes 8388608 | tf_op jit(solution)/shard_map/all_to_all | solution.py:14
  746.6 0.7 sort.32
  750.3 0.7 broadcast_select_fusion.2
  751.0 0.9 bitcast_select_fusion
  751.9 90.6 %all-to-all-done.1 = f32[64,64,256]{2,1,0:T(8,128)} async-done(((f32[64,64,256]{2,1,0:T(8,128)}), f32[64,64,256]{2,1,0:T(8,128)}, u32[]{:S(2)}, u32[]{:S(2)}) %all-to-all-start.1) | async-done | bytes 4194336 | tf_op jit(solution)/shard_map/all_to_all | solution.py:14
  842.5 12.7 %convolution_subtract_fusion = f32[256,4096]{1,0:T(8,128)} fusion(f32[256,4096]{1,0:T(8,128)} %copy-done.1, f32[256,256]{1,0:T(8,128)S(1)} %fusion.8, f32[4096,256]{1,0:T(8,128)} %bitcast.23), kind=kOutput, calls=%fused_computation.10 | convolution fusion | flops 3222274048 | bytes 12845056 | tf_op jit(solution)/shard_map/dot_general | solution.py:23
  855.2 4.9 gather_fusion.3
  860.1 4.8 broadcast_select_fusion
  (88 shorter events, 15.0 us)
Async XLA Ops:
  7.2 15.9 %copy-start = (f32[256,128]{1,0:T(8,128)S(1)}, f32[256,128]{1,0:T(8,128)}, u32[]{:S(2)}) copy-start(f32[256,128]{1,0:T(8,128)} %param.14) | copy-start | bytes 393220
  7.2 63.8 %all-reduce.8.cloned.1.call-start = ((), (), s32[]{:S(2)}) async-start(), calls=%async_computation.2 | async-start | bytes 524288 | tf_op jit(solution)/shard_map/psum | solution.py:19
  19.6 2.0 copy-start.2
  22.4 234.8 %all-reduce.14.cloned.1.call-start = ((), (), s32[]{:S(2)}) async-start(), calls=%async_computation.5 | async-start | bytes 786432 | tf_op jit(solution)/shard_map/psum | solution.py:83
  71.0 249.1 %copy-start.3 = (f32[256,256]{1,0:T(8,128)S(1)}, f32[256,256]{1,0:T(8,128)}, u32[]{:S(2)}) copy-start(f32[256,256]{1,0:T(8,128)} %all-reduce.8.cloned.1.call-done) | copy-start | bytes 786436
  323.1 11.4 %copy-start.5 = (f32[256,128]{1,0:T(8,128)S(1)}, f32[256,128]{1,0:T(8,128)}, u32[]{:S(2)}) copy-start(f32[256,128]{1,0:T(8,128)} %get-tuple-element.47) | copy-start | bytes 393220
  323.1 105.9 %all-to-all-start = ((f32[64,64,256]{2,1,0:T(8,128)}), f32[64,64,256]{2,1,0:T(8,128)}, u32[]{:S(2)}, u32[]{:S(2)}) async-start(f32[64,64,256]{2,1,0:T(8,128)} %tile.4), calls=%async_computation | async-start | bytes 8388608 | tf_op jit(solution)/shard_map/all_to_all | solution.py:14
  333.0 151.3 %all-reduce.10.cloned.1.call-start = ((), (), s32[]{:S(2)}) async-start(), calls=%async_computation.3 | async-start | bytes 524288 | tf_op jit(solution)/shard_map/psum | solution.py:19
  440.4 2.0 copy-start.1
  443.1 227.2 %all-reduce.12.cloned.1.call-start = ((), (), s32[]{:S(2)}) async-start(), calls=%async_computation.4 | async-start | bytes 786432 | tf_op jit(solution)/shard_map/psum | solution.py:83
  484.4 249.3 %copy-start.4 = (f32[256,256]{1,0:T(8,128)S(1)}, f32[256,256]{1,0:T(8,128)}, u32[]{:S(2)}) copy-start(f32[256,256]{1,0:T(8,128)} %all-reduce.10.cloned.1.call-done) | copy-start | bytes 786436
  736.6 10.9 %copy-start.6 = (f32[256,128]{1,0:T(8,128)S(1)}, f32[256,128]{1,0:T(8,128)}, u32[]{:S(2)}) copy-start(f32[256,128]{1,0:T(8,128)} %get-tuple-element.45) | copy-start | bytes 393220
  736.6 105.9 %all-to-all-start.1 = ((f32[64,64,256]{2,1,0:T(8,128)}), f32[64,64,256]{2,1,0:T(8,128)}, u32[]{:S(2)}, u32[]{:S(2)}) async-start(f32[64,64,256]{2,1,0:T(8,128)} %tile.5), calls=%async_computation.1 | async-start | bytes 8388608 | tf_op jit(solution)/shard_map/all_to_all | solution.py:14
Sparse Core Ops, SparseCore 0:
  22.5 48.4 all-reduce.7
  75.5 181.5 all-reduce.13
  443.3 41.0 all-reduce.9
  488.7 181.5 all-reduce.11
